TPU v7x, 32 devices: a whole 2x2x4 slice. The times are simulated.
32 devices in a mesh: seq: 8 (over z, x), head: 4 (over y, core).
Axes of the slice: x: 2, y: 2, z: 4, core: 2. Of those that a mesh axis runs over, the one named last changes fastest.
Arguments:
- queries: bfloat16 [1024, 16, 64], P('seq', 'head'), may hold values from -6 to 6
- keys_values: bfloat16 [1024, 16, 128], P('seq', 'head'), may hold values from -6 to 6
- out_weight: bfloat16 [16, 64, 4096], P('head'), may hold values from -1 to 1
- out_grad: bfloat16 [1024, 4096], P('seq'), may hold values from -0.75 to 0.75
- block_order: int32 [8], replicated, may hold values from 0 to 7, each once
Outputs:
- mixed_out: bfloat16 [1024, 4096], P('seq', 'head')
- grad_queries: bfloat16 [1024, 16, 64], P('seq', 'head')
- grad_keys_values: bfloat16 [1024, 16, 128], P('seq', 'head')
Inputs may be any that keep to these rules, and one draw needn't show every extreme that they name: `block_order`: A permutation of the sequence blocks 0 to 7.
All inputs are finite; a program needn't handle non-finite values.
Results may differ from a plain program's by a relative error of at most 0.03.
Values may be sent and summed in bfloat16 or wider, within the bound.
A program may use at most 64 MiB of HBM per device.

v0:
```python
import math

import jax
import jax.numpy as jnp
from jax import lax
from jax.sharding import PartitionSpec as P


def log_normalizer(scores, allowed):
    masked = jnp.where(allowed, scores, -jnp.inf)
    row_max = jnp.max(masked, axis=-1, keepdims=True)
    row_total = jnp.sum(jnp.exp(masked - row_max), axis=-1, keepdims=True)
    return (row_max + jnp.log(row_total))[..., 0]


def local(queries, keys_values, out_weight, out_grad, block_order):
    tok_rows = queries.shape[0]
    head_width = queries.shape[2]
    inv_root = 1.0 / math.sqrt(head_width)
    my_block = block_order[lax.axis_index("seq")]
    offsets = jnp.arange(tok_rows, dtype=jnp.int32)
    my_position = my_block * tok_rows + offsets
    all_position = (block_order[:, None] * tok_rows + offsets[None, :]).reshape(-1)
    gathered = lax.all_gather(keys_values, "seq", axis=0, tiled=True)
    all_keys = gathered[:, :, :head_width]
    all_values = gathered[:, :, head_width:]
    allowed = (all_position[None, :] <= my_position[:, None])[None]
    scores = (
        jnp.einsum("qhd,khd->hqk", queries, all_keys, preferred_element_type=jnp.float32) * inv_root
    )
    log_total = log_normalizer(scores, allowed)
    probs_low = jnp.where(allowed, jnp.exp(scores - log_total[:, :, None]), 0.0).astype(
        jnp.bfloat16
    )
    attended = jnp.einsum(
        "hqk,khd->qhd", probs_low, all_values, preferred_element_type=jnp.float32
    ).astype(jnp.bfloat16)
    partial_value = jnp.einsum(
        "qhd,hde->qe", attended, out_weight, preferred_element_type=jnp.float32
    )
    mixed_out = lax.psum_scatter(partial_value, "head", scatter_dimension=1, tiled=True).astype(
        jnp.bfloat16
    )
    grad_att = jnp.einsum(
        "qe,hde->qhd", out_grad, out_weight, preferred_element_type=jnp.float32
    ).astype(jnp.bfloat16)
    grad_dot = jnp.sum(grad_att.astype(jnp.float32) * attended.astype(jnp.float32), axis=2)
    dprob = jnp.einsum("qhd,khd->hqk", grad_att, all_values, preferred_element_type=jnp.float32)
    dscore = (probs_low.astype(jnp.float32) * (dprob - grad_dot.T[:, :, None])).astype(jnp.bfloat16)
    grad_queries = (
        jnp.einsum("hqk,khd->qhd", dscore, all_keys, preferred_element_type=jnp.float32) * inv_root
    ).astype(jnp.bfloat16)
    grad_keys = (
        jnp.einsum("hqk,qhd->khd", dscore, queries, preferred_element_type=jnp.float32) * inv_root
    )
    grad_values = jnp.einsum(
        "hqk,qhd->khd", probs_low, grad_att, preferred_element_type=jnp.float32
    )
    terms = jnp.concatenate([grad_keys, grad_values], axis=2)
    summed = lax.psum_scatter(terms, "seq", scatter_dimension=0, tiled=True)
    grad_keys_values = summed.astype(jnp.bfloat16)
    return (mixed_out, grad_queries, grad_keys_values)


def solution(mesh):
    return jax.shard_map(
        local,
        mesh=mesh,
        in_specs=(
            P("seq", "head", None),
            P("seq", "head", None),
            P("head", None, None),
            P("seq", None),
            P(),
        ),
        out_specs=(P("seq", "head"), P("seq", "head", None), P("seq", "head", None)),
        check_vma=False,
    )
```

profile of v0, /device:TPU:0, one launch (start us, length us, event | category | flops | bytes accessed | tf_op | source)
XLA Modules:
  0.0 167.9 jit_solution(5529985480729950572)
XLA Ops:
  7.2 0.0 copy-start
  7.2 0.0 copy-start.2
  7.2 0.0 all-gather.2.cloned.1.call-start
  7.2 1.8 %copy.8 = bf16[128,4,128]{0,2,1:T(8,128)(2,1)} copy(bf16[128,4,128]{2,1,0:T(4,128)(2,1)} %param.6) | data formatting | bytes 262144 | tf_op args[1]
  9.1 0.0 all-gather.2.cloned.1.call-update
  9.1 0.0 reduce-scatter.5.cloned.1.call-start
  9.1 1.2 dynamic_slice.3
  11.0 0.7 broadcast_multiply_fusion
  11.7 0.1 add_bitcast_fusion
  11.8 0.1 broadcast_compare_fusion
  11.9 0.0 copy-done
  11.9 1.9 %convolution_convert_fusion = bf16[128,4,64]{0,2,1:T(8,128)(2,1)S(1)} fusion(bf16[4,64,4096]{2,1,0:T(8,128)(2,1)S(1)} %copy-done, bf16[128,4096]{1,0:T(8,128)(2,1)} %param.8), kind=kOutput, calls=%fused_computation.10 | convolution fusion | flops 268468224 | bytes 3211264 | tf_op jit(solution)/shard_map/qe,hde->qhd/dot_general | solution.py:44
  13.9 39.0 %all-gather.2.cloned.1.call-done = bf16[1024,4,128]{0,2,1:T(8,128)(2,1)} async-done(((bf16[128,4,128]{0,2,1:T(8,128)(2,1)}), bf16[1024,4,128]{0,2,1:T(8,128)(2,1)}) %all-gather.2.cloned.1.call-update) | async-done | bytes 1048592 | tf_op jit(solution)/shard_map/all_gather | solution.py:24
  52.9 0.0 copy-done.2
  52.9 1.6 select_reduce_fusion
  54.6 0.6 exponential_reduce_fusion
  55.2 0.0 copy-start.1
  55.2 0.5 select_convert_fusion
  55.7 0.3 convolution_bitcast_fusion.1
  56.0 0.4 copy-done.1
  56.4 0.5 multiply_reduce_fusion
  56.9 0.5 multiply_convert_fusion
  57.4 0.3 fusion
  57.7 1.4 pad_maximum_fusion
  59.1 0.0 reduce-scatter.5.cloned.1.call-update
  59.2 0.0 reduce-scatter.3.cloned.1.call-start
  59.2 1.8 %convolution_bitcast_fusion = f32[128,4096]{1,0:T(8,128)} fusion(bf16[128,4,64]{0,2,1:T(8,128)(2,1)S(1)} %get-tuple-element.9, bf16[4,64,4096]{2,1,0:T(8,128)(2,1)S(1)} %copy-done), kind=kOutput, calls=%fused_computation | convolution fusion | flops 268435456 | bytes 4259840 | tf_op jit(solution)/shard_map/qhd,hde->qe/dot_general | solution.py:38
  61.0 0.0 reduce-scatter.3.cloned.1.call-update
  61.1 2.2 %fusion.3 = bf16[128,4,64]{0,2,1:T(8,128)(2,1)} fusion(bf16[4,128,1024]{2,1,0:T(8,128)(2,1)S(1)} %multiply_convert_fusion, bf16[1024,4,128]{0,2,1:T(8,128)(2,1)} %all-gather.2.cloned.1.call-done), kind=kOutput, calls=%fused_computation.14 | convolution fusion | flops 67174400 | bytes 1638400 | tf_op jit(solution)/shard_map/hqk,khd->qhd/dot_general | solution.py:51
  63.2 63.4 %reduce-scatter.5.cloned.1.call-done = f32[128,4,128]{0,2,1:T(8,128)} async-done(((f32[1024,4,128]{0,2,1:T(8,128)}), f32[128,4,128]{0,2,1:T(8,128)}) %reduce-scatter.5.cloned.1.call-update) | async-done | bytes 262160 | tf_op jit(solution)/shard_map/reduce_scatter | solution.py:60
  126.6 1.0 convert_element_type.47
  127.5 0.8 copy.9
  128.3 31.3 %reduce-scatter.3.cloned.1.call-done = f32[128,1024]{1,0:T(8,128)} async-done(((f32[128,4096]{1,0:T(8,128)}), f32[128,1024]{1,0:T(8,128)}) %reduce-scatter.3.cloned.1.call-update) | async-done | bytes 524304 | tf_op jit(solution)/shard_map/reduce_scatter | solution.py:41
  159.6 1.8 %convert_element_type.39 = bf16[128,1024]{1,0:T(8,128)(2,1)} convert(f32[128,1024]{1,0:T(8,128)} %reduce-scatter.3.cloned.1.call-done) | non-fusion elementwise | flops 131072 | bytes 786432 | tf_op jit(solution)/shard_map/convert_element_type | solution.py:41
  (2 shorter events, 0.0 us)
Async XLA Ops:
  7.2 4.8 %copy-start = (bf16[4,64,4096]{2,1,0:T(8,128)(2,1)S(1)}, bf16[4,64,4096]{2,1,0:T(8,128)(2,1)}, u32[]{:S(2)}) copy-start(bf16[4,64,4096]{2,1,0:T(8,128)(2,1)} %param.7) | copy-start | bytes 6291460
  7.2 45.7 %copy-start.2 = (bf16[128,4,64]{0,2,1:T(8,128)(2,1)S(1)}, bf16[128,4,64]{0,2,1:T(8,128)(2,1)}, u32[]{:S(2)}) copy-start(bf16[128,4,64]{0,2,1:T(8,128)(2,1)} %param.5) | copy-start | bytes 196612
  7.2 45.7 %all-gather.2.cloned.1.call-start = ((), (), s32[]{:S(2)}) async-start(), calls=%async_computation.2 | async-start | bytes 1179648 | tf_op jit(solution)/shard_map/all_gather | solution.py:24
  9.1 117.5 %reduce-scatter.5.cloned.1.call-start = ((), (), s32[]{:S(2)}) async-start(), calls=%async_computation.4 | async-start | bytes 2359296 | tf_op jit(solution)/shard_map/reduce_scatter | solution.py:60
  55.2 1.2 copy-start.1
  59.2 100.5 %reduce-scatter.3.cloned.1.call-start = ((), (), s32[]{:S(2)}) async-start(), calls=%async_computation.3 | async-start | bytes 2621440 | tf_op jit(solution)/shard_map/reduce_scatter | solution.py:41
Sparse Core Ops, SparseCore 0:
  10.6 42.2 all-gather.1
  59.3 67.2 reduce-scatter.4
  129.1 30.4 reduce-scatter.2
where the time goes:
time: 168 us
  waiting for transfers between devices  134 us (80%)
  between operations  14.5 us (9%)
  matrix products  9.14 us (5%)
  other arithmetic  6.13 us (4%)
  local copies, waits for them, and re-layouts  4.3 us (3%)
    reduce_scatter x1, waiting for transfers between devices, local(): summed = lax.psum_scatter(terms, 'seq', scatter_dimension=0, tiled=True)  63.4 us
    all_gather x1, waiting for transfers between devices, local(): gathered = lax.all_gather(keys_values, 'seq', axis=0, tiled=True)  39 us
    reduce_scatter x1, waiting for transfers between devices, local(): lax.psum_scatter(partial_value, 'head', scatter_dimension=1, tiled=True)  31.3 us
  transfers between devices with their start and end apart: 3, of which 3 were waited for; matrix products, arithmetic and copies ran while one was open for 6% of the time, Pallas kernels for 0%

commit v1 on v0

--- a/solution.py
+++ b/solution.py
@@ -1,9 +1,275 @@
+import functools
 import math
 
 import jax
 import jax.numpy as jnp
 from jax import lax
+from jax.experimental import pallas as pl
+from jax.experimental.pallas import tpu as pltpu
 from jax.sharding import PartitionSpec as P
+
+MESH = pl.DeviceIdType.MESH
+F32 = jnp.float32
+BF16 = jnp.bfloat16
+
+
+def dot(a, b, dims=((1,), (0,))):
+    return lax.dot_general(a, b, (dims, ((), ())), preferred_element_type=F32)
+
+
+NT = ((1,), (1,))
+
+
+def fused(
+    n, nh, hh, rows, width, inv_root,
+    q_ref, kv_ref, w_hbm, og_hbm, order_ref,
+    mixed_ref, dq_ref, dkv_ref,
+    w_ref, og_ref, kvbuf, stage, qgbuf, wbuf, probs, dscore,
+    att_out, attbuf, dq_out, dqbuf, dkv_out, dkvbuf, attfull,
+    local_sem, kv_s, kv_r, w_s, w_r, qg_s, qg_r, att_s, att_r, dq_s, dq_r, dkv_s, dkv_r,
+):
+    reps = n // hh
+    half = rows // 2
+    lanes = 2 * width
+    me = lax.axis_index("seq")
+    mh = lax.axis_index("head")
+    my_z = me // reps
+    cols = mixed_ref.shape[1]
+
+    get_w = pltpu.make_async_copy(w_hbm, w_ref, local_sem.at[0])
+    get_og = pltpu.make_async_copy(og_hbm, og_ref, local_sem.at[1])
+    get_w.start()
+    get_og.start()
+
+    def seq_at(k):
+        return lax.rem(me + (k + n), n)
+
+    def head_at(k):
+        return lax.rem(mh + (k + nh), nh)
+
+    barrier = pltpu.get_barrier_semaphore()
+    count = 0
+    for k in range(1, n):
+        pl.semaphore_signal(barrier, inc=1, device_id=(seq_at(k), mh), device_id_type=MESH)
+        count += 1
+    for j in range(hh):
+        for d in range(1, nh):
+            pl.semaphore_signal(
+                barrier, inc=1, device_id=(seq_at(reps * j), head_at(d)), device_id_type=MESH
+            )
+            count += 1
+    pl.semaphore_wait(barrier, count)
+
+    sends = []
+
+    def send(src, dst, send_sem, recv_sem, seq, head):
+        copy = pltpu.make_async_remote_copy(
+            src_ref=src, dst_ref=dst, send_sem=send_sem, recv_sem=recv_sem,
+            device_id=(seq, head), device_id_type=MESH,
+        )
+        copy.start()
+        sends.append(copy)
+
+    def arrived(dst, send_sem, recv_sem):
+        pltpu.make_async_remote_copy(
+            src_ref=dst, dst_ref=dst, send_sem=send_sem, recv_sem=recv_sem,
+            device_id=(seq_at(1), mh), device_id_type=MESH,
+        ).wait_recv()
+
+    def lane_block(i, size):
+        return pl.ds(pl.multiple_of(i * size, size), size)
+
+    for k in range(1, n):
+        to = seq_at(k)
+        send(
+            kv_ref.at[:, lane_block(to // reps, lanes)], kvbuf.at[pl.ds(k * rows, rows)],
+            kv_s.at[k], kv_r.at[k], to, mh,
+        )
+    kvbuf[0:rows, :] = kv_ref[:, lane_block(my_z, lanes)]
+    for d in range(nh - 1, 0, -1):
+        to = head_at(d)
+        send(w_hbm.at[:, lane_block(to, cols)], wbuf.at[d], w_s.at[d], w_r.at[d], me, to)
+
+    low = lax.broadcasted_iota(jnp.int32, (rows, lanes), 1) < width
+    low_half = low[:half]
+
+    get_w.wait()
+    get_og.wait()
+    gatt = dot(og_ref[...], w_ref[...], NT)
+    for pair in range(hh // 2):
+        at = slice(pair * lanes, (pair + 1) * lanes)
+        q_pair = q_ref[:, at].astype(F32)
+        g_pair = gatt[:, at]
+        stage[2 * pair] = jnp.where(low, q_pair, pltpu.roll(g_pair, width, 1)).astype(BF16)
+        stage[2 * pair + 1] = jnp.where(low, pltpu.roll(q_pair, width, 1), g_pair).astype(BF16)
+    for j in range(1, hh):
+        to = seq_at(reps * j)
+        send(stage.at[to // reps], qgbuf.at[j], qg_s.at[j], qg_r.at[j], to, mh)
+    qgbuf[0] = stage[my_z]
+
+    offsets = lax.broadcasted_iota(jnp.int32, (1, rows), 1)
+    key_pos = jnp.concatenate(
+        [order_ref[seq_at(-k)] * rows + offsets for k in range(n)], axis=1
+    )
+    row_iota = lax.broadcasted_iota(jnp.int32, (rows, 1), 0)
+
+    def pack(x):
+        return jnp.where(low_half, x[:half], pltpu.roll(x[half:], width, 1)).astype(BF16)
+
+    def pack_high(x):
+        return jnp.where(low_half, pltpu.roll(x[:half], width, 1), x[half:]).astype(BF16)
+
+    for k in range(1, n):
+        arrived(kvbuf.at[pl.ds(k * rows, rows)], kv_s.at[k], kv_r.at[k])
+
+    for j in range(hh):
+        owner = seq_at(-reps * j)
+        if j > 0:
+            arrived(qgbuf.at[j], qg_s.at[j], qg_r.at[j])
+        qg = qgbuf[j]
+        zero = jnp.zeros_like(qg)
+        kv = kvbuf[...]
+        scores = dot(jnp.where(low, qg, zero), kv, NT) * inv_root
+        allowed = key_pos <= order_ref[owner] * rows + row_iota
+        scores = jnp.where(allowed, scores, -jnp.inf)
+        e = jnp.exp(scores - jnp.max(scores, axis=1, keepdims=True))
+        p = (e * (1.0 / jnp.sum(e, axis=1, keepdims=True))).astype(BF16)
+        probs[j * rows:(j + 1) * rows, :] = p
+        att = dot(p, kv)
+        att_out[j] = pack_high(att)
+        for d in range(nh):
+            if d == 0 and j == 0:
+                attbuf[0, my_z] = att_out[0]
+            else:
+                send(
+                    att_out.at[j], attbuf.at[d, my_z], att_s.at[d, j], att_r.at[d, j],
+                    owner, head_at(d),
+                )
+        dprob = dot(jnp.where(low, zero, qg), kv, NT)
+        grad_dot = jnp.sum(
+            jnp.where(low, 0.0, qg.astype(F32) * att.astype(BF16).astype(F32)),
+            axis=1, keepdims=True,
+        )
+        ds = (p.astype(F32) * (dprob - grad_dot)).astype(BF16)
+        dscore[j * rows:(j + 1) * rows, :] = ds
+        dq_out[j] = pack(dot(ds, kv) * inv_root)
+        if j == 0:
+            dqbuf[my_z] = dq_out[0]
+        else:
+            send(dq_out.at[j], dqbuf.at[my_z], dq_s.at[j], dq_r.at[j], owner, mh)
+
+    qg_all = qgbuf[...].reshape(hh * rows, lanes)
+    qgt = jnp.transpose(qg_all.astype(F32)).astype(BF16)
+    grad_k = dot(qgt, dscore[...]) * inv_root
+    grad_v = dot(qgt, probs[...])
+    upper = lax.broadcasted_iota(jnp.int32, (lanes, rows), 0) < width
+    for k in [*range(1, n), 0]:
+        at = slice(k * rows, (k + 1) * rows)
+        dkv_out[k] = jnp.transpose(jnp.where(upper, grad_k[:, at], grad_v[:, at])).astype(BF16)
+        if k == 0:
+            dkvbuf[0] = dkv_out[0]
+        else:
+            send(dkv_out.at[k], dkvbuf.at[k], dkv_s.at[k], dkv_r.at[k], seq_at(-k), mh)
+
+    def unpack(first, second):
+        first, second = first.astype(F32), second.astype(F32)
+        top = jnp.where(low_half, first, pltpu.roll(second, width, 1)).astype(BF16)
+        bottom = jnp.where(low_half, pltpu.roll(first, width, 1), second).astype(BF16)
+        return top, bottom
+
+    for j in range(1, hh):
+        arrived(dqbuf.at[(my_z + j) % hh], dq_s.at[j], dq_r.at[j])
+    for pair in range(hh // 2):
+        at = slice(pair * lanes, (pair + 1) * lanes)
+        top, bottom = unpack(dqbuf[2 * pair], dqbuf[2 * pair + 1])
+        dq_ref[0:half, at] = top
+        dq_ref[half:rows, at] = bottom
+
+    total = None
+    for d in range(nh):
+        for j in range(hh):
+            if d or j:
+                arrived(attbuf.at[d, (my_z + j) % hh], att_s.at[d, j], att_r.at[d, j])
+        for pair in range(hh // 2):
+            at = slice(pair * lanes, (pair + 1) * lanes)
+            top, bottom = unpack(attbuf[d, 2 * pair], attbuf[d, 2 * pair + 1])
+            attfull[d, 0:half, at] = top
+            attfull[d, half:rows, at] = bottom
+        if d == 0:
+            weight = w_ref[:, lane_block(mh, cols)]
+        else:
+            arrived(wbuf.at[d], w_s.at[d], w_r.at[d])
+            weight = wbuf[d]
+        term = dot(attfull[d], weight)
+        total = term if total is None else total + term
+    mixed_ref[...] = total.astype(BF16)
+
+    for k in range(1, n):
+        arrived(dkvbuf.at[k], dkv_s.at[k], dkv_r.at[k])
+    for z in range(hh):
+        acc = None
+        for r in range(reps):
+            term = dkvbuf[lax.rem(z * reps + r + n - me, n)].astype(F32)
+            acc = term if acc is None else acc + term
+        dkv_ref[:, z * lanes:(z + 1) * lanes] = acc.astype(BF16)
+
+    for copy in sends:
+        copy.wait_send()
+
+
+def fused_local(n, nh, queries, keys_values, out_weight, out_grad, block_order):
+    rows, hh, width = queries.shape
+    lanes = 2 * width
+    depth = out_grad.shape[1]
+    cols = depth // nh
+    half = rows // 2
+    vmem = pl.BlockSpec(memory_space=pltpu.VMEM)
+    hbm = pl.BlockSpec(memory_space=pl.ANY)
+    dma = pltpu.SemaphoreType.DMA
+    mixed, dq, dkv = pl.pallas_call(
+        functools.partial(fused, n, nh, hh, rows, width, 1.0 / math.sqrt(width)),
+        out_shape=(
+            jax.ShapeDtypeStruct((rows, cols), BF16),
+            jax.ShapeDtypeStruct((rows, hh * width), BF16),
+            jax.ShapeDtypeStruct((rows, hh * lanes), BF16),
+        ),
+        in_specs=[vmem, vmem, hbm, hbm, pl.BlockSpec(memory_space=pltpu.SMEM)],
+        out_specs=(vmem, vmem, vmem),
+        scratch_shapes=[
+            pltpu.VMEM((hh * width, depth), BF16),
+            pltpu.VMEM((rows, depth), BF16),
+            pltpu.VMEM((n * rows, lanes), BF16),
+            pltpu.VMEM((hh, rows, lanes), BF16),
+            pltpu.VMEM((hh, rows, lanes), BF16),
+            pltpu.VMEM((nh, hh * width, cols), BF16),
+            pltpu.VMEM((hh * rows, n * rows), BF16),
+            pltpu.VMEM((hh * rows, n * rows), BF16),
+            pltpu.VMEM((hh, half, lanes), BF16),
+            pltpu.VMEM((nh, hh, half, lanes), BF16),
+            pltpu.VMEM((hh, half, lanes), BF16),
+            pltpu.VMEM((hh, half, lanes), BF16),
+            pltpu.VMEM((n, rows, lanes), BF16),
+            pltpu.VMEM((n, rows, lanes), BF16),
+            pltpu.VMEM((nh, rows, hh * width), BF16),
+            dma((2,)),
+            dma((n,)), dma((n,)),
+            dma((nh,)), dma((nh,)),
+            dma((hh,)), dma((hh,)),
+            dma((nh, hh)), dma((nh, hh)),
+            dma((hh,)), dma((hh,)),
+            dma((n,)), dma((n,)),
+        ],
+        compiler_params=pltpu.CompilerParams(
+            collective_id=0, has_side_effects=True, vmem_limit_bytes=48 * 2**20
+        ),
+    )(
+        queries.reshape(rows, hh * width),
+        keys_values.reshape(rows, hh * lanes),
+        out_weight.reshape(hh * width, depth),
+        out_grad,
+        block_order,
+    )
+    return mixed, dq.reshape(queries.shape), dkv.reshape(keys_values.shape)
 
 
 def log_normalizer(scores, allowed):
@@ -63,8 +329,17 @@
 
 
 def solution(mesh):
+    n, nh = mesh.shape["seq"], mesh.shape["head"]
+
+    def step(queries, keys_values, out_weight, out_grad, block_order):
+        rows, hh, width = queries.shape
+        fits = hh % 2 == 0 and n % hh == 0 and 2 * width == 128 and rows % 32 == 0
+        if fits and 8 * n * rows * hh * rows < 2**23:
+            return fused_local(n, nh, queries, keys_values, out_weight, out_grad, block_order)
+        return local(queries, keys_values, out_weight, out_grad, block_order)
+
     return jax.shard_map(
-        local,
+        step,
         mesh=mesh,
         in_specs=(
             P("seq", "head", None),

time: 168 us -> 43.6 us (0.26)
  waiting for transfers between devices: 134 us -> 0 us
  Pallas kernels: 0 us -> 35.3 us
  between operations: 14.5 us -> 0.66 us
  matrix products: 9.14 us -> 0 us
  other arithmetic: 6.13 us -> 0 us
  local copies, waits for them, and re-layouts: 4.3 us -> 7.46 us
    reduce_scatter x2 -> x0, waiting for transfers between devices: 94.6 us -> none  [the longest x1 63.4 us: local(): summed = lax.psum_scatter(terms, 'seq', scatter_dimension=0, tiled=True)]
    all_gather x1 -> x0, waiting for transfers between devices: 39 us -> none  [local(): gathered = lax.all_gather(keys_values, 'seq', axis=0, tiled=True)]
    pallas_call x0 -> x1, Pallas kernels: none -> 35.3 us  [fused_local(): pl.pallas_call(functools.partial(fused, n, nh, hh, rows, width, 1.0 / mat...]
    dot_general x8 -> x0, matrix products: 9.14 us -> none  [the longest x1 2.16 us: local(): jnp.einsum('hqk,khd->qhd', dscore, all_keys, preferred_element_type=jnp.f...]
    convert_element_type x3 -> x0, other arithmetic: 3.22 us -> none  [the longest x1 1.78 us: local(): lax.psum_scatter(partial_value, 'head', scatter_dimension=1, tiled=True)]
    unnamed x8, local copies, waits for them, and re-layouts: 3.06 us -> 5.09 us
  transfers between devices with their start and end apart: 3 -> 0, of which waited for: 3 -> 0; matrix products, arithmetic and copies ran while one was open for 6% -> 0% of each run, Pallas kernels for 0% -> 0%
where the time goes in v1:
time: 43.6 us; the launch traced here: 43.4 us
  Pallas kernels  35.3 us (81%)
  local copies, waits for them, and re-layouts  7.46 us (17%)
  between operations  0.66 us (2%)
    pallas_call x1, Pallas kernels, fused_local(): pl.pallas_call(functools.partial(fused, n, nh, hh, rows, width, 1.0 / mat...  35.3 us
    unnamed x8, local copies, waits for them, and re-layouts  5.09 us
    reshape x1, local copies, waits for them, and re-layouts, fused_local(): queries.reshape(rows, hh * width)  0.94 us

profile of v1, /device:TPU:0, one launch (start us, length us, event | category | flops | bytes accessed | tf_op | source)
XLA Modules:
  0.0 43.4 jit_solution(2817896922430025220)
XLA Ops:
  0.6 0.9 %copy.10.q_ref = bf16[128,256]{1,0:T(8,128)(2,1)S(1)} copy(bf16[128,256]{0,1:T(8,128)(2,1)} %bitcast.10) | data formatting | bytes 131072 | tf_op jit(solution)/shard_map/reshape | solution.py:266
  1.6 0.9 %copy.14 = bf16[16,8,4,128]{3,1,2,0:T(8,128)(2,1)S(1)} copy(bf16[16,8,4,128]{3,2,1,0:T(4,128)(2,1)} %bitcast.9) | data formatting | bytes 262144
  2.5 0.0 copy-start
  2.5 1.6 %copy-done = bf16[4,64,4096]{2,1,0:T(8,128)(2,1)S(1)} copy-done((bf16[4,64,4096]{2,1,0:T(8,128)(2,1)S(1)}, bf16[4,64,4096]{2,1,0:T(8,128)(2,1)}, u32[]{:S(2)}) %copy-start) | copy-done | bytes 2097176
  4.1 0.0 copy-start.1
  4.1 1.2 %copy-done.1 = bf16[128,4096]{1,0:T(8,128)(2,1)S(1)} copy-done((bf16[128,4096]{1,0:T(8,128)(2,1)S(1)}, bf16[128,4096]{1,0:T(8,128)(2,1)}, u32[]{:S(2)}) %copy-start.1) | copy-done | bytes 1048600
  5.3 0.0 copy-start.2
  5.3 0.7 %copy-done.2 = s32[8]{0:T(128)S(1)} copy-done((s32[8]{0:T(128)S(1)}, s32[8]{0:T(128)}, u32[]{:S(2)}) %copy-start.2) | copy-done | bytes 56
  6.0 35.3 %shard_map.76 = (bf16[128,1024]{1,0:T(8,128)(2,1)S(1)}, bf16[128,256]{1,0:T(8,128)(2,1)S(1)}, bf16[128,512]{1,0:T(8,128)(2,1)S(1)}) custom-call(bf16[128,256]{1,0:T(8,128)(2,1)S(1)} %copy.10.q_ref, bf16[128,512]{1,0:T(8,128)(2,1)S(1)} %bitcast.8, bf16[256,4096]{1,0:T(8,128)(2,1)S(1)} %bitcast.7, bf16[128,4096]{1,0:T(8,128)(2,1)S(1)} %copy-done.1, s32[8]{0:T(128)S(1)} %copy-done.2), custom_call_target="tpu_custom_call" | custom-call | tf_op jit(solution)/shard_map/pallas_call | solution.py:229
  41.2 0.7 %copy.11 = bf16[128,256]{0,1:T(8,128)(2,1)} copy(bf16[128,256]{1,0:T(8,128)(2,1)S(1)} %get-tuple-element.7) | data formatting | bytes 131072 | tf_op jit(solution)/shard_map/pallas_call | solution.py:229
  42.0 0.7 %reshape.25 = bf16[128,4,128]{2,1,0:T(4,128)(2,1)} reshape(bf16[128,512]{1,0:T(8,128)(2,1)S(1)} %get-tuple-element.8) | data formatting | bytes 262144 | tf_op jit(solution)/shard_map/reshape | solution.py:272
  42.7 0.7 %copy.16 = bf16[128,1024]{1,0:T(8,128)(2,1)} copy(bf16[128,1024]{1,0:T(8,128)(2,1)S(1)} %get-tuple-element.15) | data formatting | bytes 524288
Async XLA Ops:
  2.5 1.6 %copy-start = (bf16[4,64,4096]{2,1,0:T(8,128)(2,1)S(1)}, bf16[4,64,4096]{2,1,0:T(8,128)(2,1)}, u32[]{:S(2)}) copy-start(bf16[4,64,4096]{2,1,0:T(8,128)(2,1)} %param.7) | copy-start | bytes 6291460
  4.1 1.2 %copy-start.1 = (bf16[128,4096]{1,0:T(8,128)(2,1)S(1)}, bf16[128,4096]{1,0:T(8,128)(2,1)}, u32[]{:S(2)}) copy-start(bf16[128,4096]{1,0:T(8,128)(2,1)} %og_hbm.1) | copy-start | bytes 3145732
  5.3 0.7 %copy-start.2 = (s32[8]{0:T(128)S(1)}, s32[8]{0:T(128)}, u32[]{:S(2)}) copy-start(s32[8]{0:T(128)} %order_ref.1) | copy-start | bytes 100

commit v2 on v1

v2 whole, which is shorter than its diff:
```python
import functools
import math

import jax
import jax.numpy as jnp
from jax import lax
from jax.experimental import pallas as pl
from jax.experimental.pallas import tpu as pltpu
from jax.sharding import PartitionSpec as P

MESH = pl.DeviceIdType.MESH
F32 = jnp.float32
BF16 = jnp.bfloat16
PIECES = 2


def dot(a, b, dims=((1,), (0,))):
    return lax.dot_general(a, b, (dims, ((), ())), preferred_element_type=F32)


NT = ((1,), (1,))


def fused(
    n, nh, hh, rows, width, inv_root,
    q_hbm, kv_hbm, w_hbm, og_hbm, order_ref,
    mixed_ref, dq_ref, dkv_ref,
    q_ref, kv_ref, w_ref, og_ref, kvstage, kvbuf, kvt, stage, qgbuf, wbuf, probs, dscore,
    att_out, attbuf, dq_out, dqbuf, dkv_out, dkvbuf,
    local_sem, kv_s, kv_r, w_s, w_r, f_s, f_r,
    qg_s, qg_r, att_s, att_r, dq_s, dq_r, dkv_s, dkv_r,
):
    reps = n // hh
    lanes = 2 * width
    me = lax.axis_index("seq")
    mh = lax.axis_index("head")
    my_z = me // reps
    my_r = lax.rem(me, reps)
    my_y, my_c = mh // 2, lax.rem(mh, 2)
    n_y = nh // 2
    cols = mixed_ref.shape[1]
    w_rows = hh * width
    share = w_rows // reps
    piece = share // PIECES

    loads = [
        pltpu.make_async_copy(src, dst, local_sem.at[i])
        for i, (src, dst) in enumerate(
            [(kv_hbm, kv_ref), (w_hbm, w_ref), (og_hbm, og_ref), (q_hbm, q_ref)]
        )
    ]
    for load in loads:
        load.start()

    def seq_at(k):
        return lax.rem(me + (k + n), n)

    def head_at(d, sign=1):
        y = lax.rem(my_y + (sign * (d // 2) + n_y), n_y)
        return y * 2 + lax.rem(my_c + d % 2, 2)

    def side_at(r):
        return my_z * reps + lax.rem(my_r + (r + reps), reps)

    barrier = pltpu.get_barrier_semaphore()
    count = 0
    for k in range(1, n):
        pl.semaphore_signal(barrier, inc=1, device_id=(seq_at(k), mh), device_id_type=MESH)
        count += 1
    for j in range(hh):
        for d in range(1, nh):
            pl.semaphore_signal(
                barrier, inc=1, device_id=(seq_at(reps * j), head_at(d, -1)), device_id_type=MESH
            )
            count += 1
    loads[0].wait()
    for z in range(hh):
        kvstage[z] = kv_ref[:, z, :]
    pl.semaphore_wait(barrier, count)

    sends = []

    def send(src, dst, send_sem, recv_sem, seq, head):
        copy = pltpu.make_async_remote_copy(
            src_ref=src, dst_ref=dst, send_sem=send_sem, recv_sem=recv_sem,
            device_id=(seq, head), device_id_type=MESH,
        )
        copy.start()
        sends.append(copy)

    def arrived(dst, send_sem, recv_sem):
        pltpu.make_async_remote_copy(
            src_ref=dst, dst_ref=dst, send_sem=send_sem, recv_sem=recv_sem,
            device_id=(seq_at(1), mh), device_id_type=MESH,
        ).wait_recv()

    def w_part(r, i):
        return pl.ds(pl.multiple_of(r * share + i * piece, piece), piece)

    for k in range(1, n):
        to = seq_at(k)
        send(
            kvstage.at[to // reps], kvbuf.at[pl.ds(k * rows, rows)],
            kv_s.at[k], kv_r.at[k], to, mh,
        )
    far = [(i, d) for i in range(PIECES) for d in range(2, nh)]
    for i, d in far:
        to = head_at(d)
        at = pl.ds(pl.multiple_of(to * cols, cols), cols)
        send(
            w_hbm.at[w_part(my_r, i), at], wbuf.at[d, w_part(my_r, i)],
            w_s.at[d, i], w_r.at[d, i], me, to,
        )
    at = pl.ds(pl.multiple_of(head_at(1) * cols, cols), cols)
    send(w_hbm.at[:, at], wbuf.at[1], w_s.at[1, 0], w_r.at[1, 0], me, head_at(1))

    def forward(i, d):
        part = wbuf.at[d, w_part(my_r, i)]
        arrived(part, w_s.at[d, i], w_r.at[d, i])
        for r in range(1, reps):
            send(part, part, f_s.at[d, i, r], f_r.at[d, i, r], side_at(r), mh)

    kvbuf[0:rows, :] = kvstage[my_z]
    kvt[:, 0:rows] = jnp.transpose(kvstage[my_z].astype(F32)).astype(BF16)

    loads[1].wait()
    loads[2].wait()
    loads[3].wait()
    gatt = dot(w_ref[...], og_ref[...], NT).astype(BF16)
    for z in range(hh):
        at = slice(z * width, (z + 1) * width)
        stage[z, 0:width] = q_ref[at]
        stage[z, width:lanes] = gatt[at]
    for j in range(1, hh):
        to = seq_at(reps * j)
        send(stage.at[to // reps], qgbuf.at[j], qg_s.at[j], qg_r.at[j], to, mh)
    qgbuf[0] = stage[my_z]

    offsets = lax.broadcasted_iota(jnp.int32, (1, rows), 1)
    key_pos = jnp.concatenate(
        [order_ref[seq_at(-k)] * rows + offsets for k in range(n)], axis=1
    )
    row_iota = lax.broadcasted_iota(jnp.int32, (rows, 1), 0)
    low = lax.broadcasted_iota(jnp.int32, (rows, lanes), 1) < width

    for step, (i, d) in enumerate(far):
        if step < len(far) // 2:
            forward(i, d)
    for k in range(1, n):
        at = slice(k * rows, (k + 1) * rows)
        arrived(kvbuf.at[pl.ds(k * rows, rows)], kv_s.at[k], kv_r.at[k])
        kvt[:, at] = jnp.transpose(kvbuf[at, :].astype(F32)).astype(BF16)
    ahead = far[len(far) // 2:]

    for j in range(hh):
        owner = seq_at(-reps * j)
        if j > 0:
            arrived(qgbuf.at[j], qg_s.at[j], qg_r.at[j])
        qg = jnp.transpose(qgbuf[j].astype(F32))
        grad_rows = jnp.where(low, 0.0, qg)
        scores = dot(jnp.where(low, qg, 0.0).astype(BF16), kvt[...]) * inv_root
        allowed = key_pos <= order_ref[owner] * rows + row_iota
        scores = jnp.where(allowed, scores, -jnp.inf)
        e = jnp.exp(scores - jnp.max(scores, axis=1, keepdims=True))
        p = (e * (1.0 / jnp.sum(e, axis=1, keepdims=True))).astype(BF16)
        probs[j * rows:(j + 1) * rows, :] = p
        att = dot(p, kvbuf[...])
        att_out[j] = jnp.transpose(att)[width:].astype(BF16)
        my_rows = pl.ds(pl.multiple_of(my_z * width, width), width)
        for d in range(nh):
            if d == 0 and j == 0:
                attbuf[0, my_rows, :] = att_out[0]
            else:
                send(
                    att_out.at[j], attbuf.at[d, my_rows], att_s.at[d, j], att_r.at[d, j],
                    owner, head_at(d),
                )
        dprob = dot(grad_rows.astype(BF16), kvt[...])
        grad_dot = jnp.sum(grad_rows * att.astype(BF16).astype(F32), axis=1, keepdims=True)
        ds = (p.astype(F32) * (dprob - grad_dot)).astype(BF16)
        dscore[j * rows:(j + 1) * rows, :] = ds
        dq_out[j] = jnp.transpose(dot(ds, kvbuf[...]) * inv_root)[:width].astype(BF16)
        if j == 0:
            dqbuf[my_rows, :] = dq_out[0]
        else:
            send(dq_out.at[j], dqbuf.at[my_rows], dq_s.at[j], dq_r.at[j], owner, mh)
        for i, d in ahead[j * len(ahead) // hh:(j + 1) * len(ahead) // hh]:
            forward(i, d)

    qgt = jnp.concatenate([qgbuf[j] for j in range(hh)], axis=1)
    grad_k = dot(qgt, dscore[...]) * inv_root
    grad_v = dot(qgt, probs[...])
    upper = lax.broadcasted_iota(jnp.int32, (lanes, rows), 0) < width
    for k in [*range(1, n), 0]:
        at = slice(k * rows, (k + 1) * rows)
        dkv_out[k] = jnp.transpose(jnp.where(upper, grad_k[:, at], grad_v[:, at])).astype(BF16)
        if k == 0:
            dkvbuf[0] = dkv_out[0]
        else:
            send(dkv_out.at[k], dkvbuf.at[k], dkv_s.at[k], dkv_r.at[k], seq_at(-k), mh)

    def z_rows(j):
        z = lax.rem(my_z + j, hh)
        return pl.ds(pl.multiple_of(z * width, width), width)

    for j in range(1, hh):
        arrived(dqbuf.at[z_rows(j)], dq_s.at[j], dq_r.at[j])
    dq_ref[...] = dqbuf[...]

    total = None
    for d in range(nh):
        for j in range(hh):
            if d or j:
                arrived(attbuf.at[d, z_rows(j)], att_s.at[d, j], att_r.at[d, j])
        if d == 0:
            weight = w_ref[:, pl.ds(pl.multiple_of(mh * cols, cols), cols)]
        else:
            if d == 1:
                arrived(wbuf.at[1], w_s.at[1, 0], w_r.at[1, 0])
            else:
                for i in range(PIECES):
                    for r in range(1, reps):
                        source = lax.rem(my_r + (reps - r), reps)
                        arrived(
                            wbuf.at[d, w_part(source, i)], f_s.at[d, i, r], f_r.at[d, i, r]
                        )
            weight = wbuf[d]
        att_rows = jnp.transpose(attbuf[d].astype(F32)).astype(BF16)
        term = dot(att_rows, weight)
        total = term if total is None else total + term
    mixed_ref[...] = total.astype(BF16)

    for k in range(1, n):
        arrived(dkvbuf.at[k], dkv_s.at[k], dkv_r.at[k])
    for z in range(hh):
        acc = None
        for r in range(reps):
            term = dkvbuf[lax.rem(z * reps + r + n - me, n)].astype(F32)
            acc = term if acc is None else acc + term
        dkv_ref[:, z, :] = acc.astype(BF16)

    for copy in sends:
        copy.wait_send()


def fused_local(n, nh, queries, keys_values, out_weight, out_grad, block_order):
    rows, hh, width = queries.shape
    lanes = 2 * width
    depth = out_grad.shape[1]
    cols = depth // nh
    reps = n // hh
    vmem = pl.BlockSpec(memory_space=pltpu.VMEM)
    hbm = pl.BlockSpec(memory_space=pl.ANY)
    dma = pltpu.SemaphoreType.DMA
    mixed, dq, dkv = pl.pallas_call(
        functools.partial(fused, n, nh, hh, rows, width, 1.0 / math.sqrt(width)),
        out_shape=(
            jax.ShapeDtypeStruct((rows, cols), BF16),
            jax.ShapeDtypeStruct((hh * width, rows), BF16),
            jax.ShapeDtypeStruct((rows, hh, lanes), BF16),
        ),
        in_specs=[hbm, hbm, hbm, hbm, pl.BlockSpec(memory_space=pltpu.SMEM)],
        out_specs=(vmem, vmem, vmem),
        scratch_shapes=[
            pltpu.VMEM((hh * width, rows), BF16),
            pltpu.VMEM((rows, hh, lanes), BF16),
            pltpu.VMEM((hh * width, depth), BF16),
            pltpu.VMEM((rows, depth), BF16),
            pltpu.VMEM((hh, rows, lanes), BF16),
            pltpu.VMEM((n * rows, lanes), BF16),
            pltpu.VMEM((lanes, n * rows), BF16),
            pltpu.VMEM((hh, lanes, rows), BF16),
            pltpu.VMEM((hh, lanes, rows), BF16),
            pltpu.VMEM((nh, hh * width, cols), BF16),
            pltpu.VMEM((hh * rows, n * rows), BF16),
            pltpu.VMEM((hh * rows, n * rows), BF16),
            pltpu.VMEM((hh, width, rows), BF16),
            pltpu.VMEM((nh, hh * width, rows), BF16),
            pltpu.VMEM((hh, width, rows), BF16),
            pltpu.VMEM((hh * width, rows), BF16),
            pltpu.VMEM((n, rows, lanes), BF16),
            pltpu.VMEM((n, rows, lanes), BF16),
            dma((4,)),
            dma((n,)), dma((n,)),
            dma((nh, PIECES)), dma((nh, PIECES)),
            dma((nh, PIECES, reps)), dma((nh, PIECES, reps)),
            dma((hh,)), dma((hh,)),
            dma((nh, hh)), dma((nh, hh)),
            dma((hh,)), dma((hh,)),
            dma((n,)), dma((n,)),
        ],
        compiler_params=pltpu.CompilerParams(
            collective_id=0, has_side_effects=True, vmem_limit_bytes=60 * 2**20
        ),
    )(
        jnp.transpose(queries, (1, 2, 0)).reshape(hh * width, rows),
        keys_values,
        out_weight.reshape(hh * width, depth),
        out_grad,
        block_order,
    )
    dq = jnp.transpose(dq.reshape(hh, width, rows), (2, 0, 1))
    return mixed, dq, dkv


def log_normalizer(scores, allowed):
    masked = jnp.where(allowed, scores, -jnp.inf)
    row_max = jnp.max(masked, axis=-1, keepdims=True)
    row_total = jnp.sum(jnp.exp(masked - row_max), axis=-1, keepdims=True)
    return (row_max + jnp.log(row_total))[..., 0]


def local(queries, keys_values, out_weight, out_grad, block_order):
    tok_rows = queries.shape[0]
    head_width = queries.shape[2]
    inv_root = 1.0 / math.sqrt(head_width)
    my_block = block_order[lax.axis_index("seq")]
    offsets = jnp.arange(tok_rows, dtype=jnp.int32)
    my_position = my_block * tok_rows + offsets
    all_position = (block_order[:, None] * tok_rows + offsets[None, :]).reshape(-1)
    gathered = lax.all_gather(keys_values, "seq", axis=0, tiled=True)
    all_keys = gathered[:, :, :head_width]
    all_values = gathered[:, :, head_width:]
    allowed = (all_position[None, :] <= my_position[:, None])[None]
    scores = (
        jnp.einsum("qhd,khd->hqk", queries, all_keys, preferred_element_type=jnp.float32) * inv_root
    )
    log_total = log_normalizer(scores, allowed)
    probs_low = jnp.where(allowed, jnp.exp(scores - log_total[:, :, None]), 0.0).astype(
        jnp.bfloat16
    )
    attended = jnp.einsum(
        "hqk,khd->qhd", probs_low, all_values, preferred_element_type=jnp.float32
    ).astype(jnp.bfloat16)
    partial_value = jnp.einsum(
        "qhd,hde->qe", attended, out_weight, preferred_element_type=jnp.float32
    )
    mixed_out = lax.psum_scatter(partial_value, "head", scatter_dimension=1, tiled=True).astype(
        jnp.bfloat16
    )
    grad_att = jnp.einsum(
        "qe,hde->qhd", out_grad, out_weight, preferred_element_type=jnp.float32
    ).astype(jnp.bfloat16)
    grad_dot = jnp.sum(grad_att.astype(jnp.float32) * attended.astype(jnp.float32), axis=2)
    dprob = jnp.einsum("qhd,khd->hqk", grad_att, all_values, preferred_element_type=jnp.float32)
    dscore = (probs_low.astype(jnp.float32) * (dprob - grad_dot.T[:, :, None])).astype(jnp.bfloat16)
    grad_queries = (
        jnp.einsum("hqk,khd->qhd", dscore, all_keys, preferred_element_type=jnp.float32) * inv_root
    ).astype(jnp.bfloat16)
    grad_keys = (
        jnp.einsum("hqk,qhd->khd", dscore, queries, preferred_element_type=jnp.float32) * inv_root
    )
    grad_values = jnp.einsum(
        "hqk,qhd->khd", probs_low, grad_att, preferred_element_type=jnp.float32
    )
    terms = jnp.concatenate([grad_keys, grad_values], axis=2)
    summed = lax.psum_scatter(terms, "seq", scatter_dimension=0, tiled=True)
    grad_keys_values = summed.astype(jnp.bfloat16)
    return (mixed_out, grad_queries, grad_keys_values)


def solution(mesh):
    n, nh = mesh.shape["seq"], mesh.shape["head"]

    def step(queries, keys_values, out_weight, out_grad, block_order):
        rows, hh, width = queries.shape
        fits = nh % 2 == 0 and n % hh == 0 and width == 64 and rows % 128 == 0
        if fits and 8 * n * rows * hh * rows < 2**23:
            return fused_local(n, nh, queries, keys_values, out_weight, out_grad, block_order)
        return local(queries, keys_values, out_weight, out_grad, block_order)

    return jax.shard_map(
        step,
        mesh=mesh,
        in_specs=(
            P("seq", "head", None),
            P("seq", "head", None),
            P("head", None, None),
            P("seq", None),
            P(),
        ),
        out_specs=(P("seq", "head"), P("seq", "head", None), P("seq", "head", None)),
        check_vma=False,
    )
```

time: 43.6 us -> 41 us (0.940)
  local copies, waits for them, and re-layouts: 7.46 us -> 4.75 us
    reshape x2 -> x0, local copies, waits for them, and re-layouts: 1.63 us -> none  [the longest x1 0.94 us: fused_local(): queries.reshape(rows, hh * width)]
    pallas_call x1 -> x0, local copies, waits for them, and re-layouts: 0.73 us -> none  [fused_local(): pl.pallas_call(functools.partial(fused, n, nh, hh, rows, width, 1.0 / mat...]
    unnamed x8 -> x3, local copies, waits for them, and re-layouts: 5.09 us -> 4.75 us
where the time goes in v2:
time: 41 us; the launch traced here: 40.8 us
  Pallas kernels  35.4 us (86%)
  local copies, waits for them, and re-layouts  4.75 us (12%)
  between operations  0.64 us (2%)
    pallas_call x1, Pallas kernels, fused_local(): pl.pallas_call(functools.partial(fused, n, nh, hh, rows, width, 1.0 / mat...  35.4 us
    unnamed x3, local copies, waits for them, and re-layouts  4.75 us

profile of v2, /device:TPU:0, one launch (start us, length us, event | category | flops | bytes accessed | tf_op | source)
XLA Modules:
  0.0 40.8 jit_solution(174133919061293543)
XLA Ops:
  0.6 35.4 %shard_map.76 = (bf16[128,1024]{1,0:T(8,128)(2,1)}, bf16[256,128]{1,0:T(8,128)(2,1)}, bf16[128,4,128]{2,1,0:T(4,128)(2,1)}) custom-call(bf16[256,128]{1,0:T(8,128)(2,1)} %bitcast.8, bf16[128,4,128]{2,1,0:T(4,128)(2,1)} %kv_hbm.1, bf16[256,4096]{1,0:T(8,128)(2,1)} %bitcast.7, bf16[128,4096]{1,0:T(8,128)(2,1)} %og_hbm.1, s32[8]{0:T(128)} %order_ref.1), custom_call_target="tpu_custom_call" | custom-call | tf_op jit(solution)/shard_map/pallas_call | solution.py:255
  36.0 1.7 %copy.11 = bf16[128,1024]{1,0:T(8,128)(2,1)} copy(bf16[128,1024]{1,0:T(8,128)(2,1)} %get-tuple-element.12) | data formatting | bytes 524288
  37.7 1.5 %copy.12 = bf16[128,4,64]{0,2,1:T(8,128)(2,1)} copy(bf16[128,4,64]{0,2,1:T(8,128)(2,1)} %bitcast.9) | data formatting | bytes 131072
  39.2 1.6 %copy.13 = bf16[128,4,128]{2,1,0:T(4,128)(2,1)} copy(bf16[128,4,128]{2,1,0:T(4,128)(2,1)} %get-tuple-element.14) | data formatting | bytes 262144

commit v3 on v2

--- a/solution.py
+++ b/solution.py
@@ -12,6 +12,7 @@
 F32 = jnp.float32
 BF16 = jnp.bfloat16
 PIECES = 2
+VLIM = 952
 
 
 def dot(a, b, dims=((1,), (0,))):
@@ -26,9 +27,9 @@
     q_hbm, kv_hbm, w_hbm, og_hbm, order_ref,
     mixed_ref, dq_ref, dkv_ref,
     q_ref, kv_ref, w_ref, og_ref, kvstage, kvbuf, kvt, stage, qgbuf, wbuf, probs, dscore,
-    att_out, attbuf, dq_out, dqbuf, dkv_out, dkvbuf,
+    attbuf, home_out, homebuf, dkv_out, dkvbuf,
     local_sem, kv_s, kv_r, w_s, w_r, f_s, f_r,
-    qg_s, qg_r, att_s, att_r, dq_s, dq_r, dkv_s, dkv_r,
+    qg_s, qg_r, att_s, att_r, home_s, home_r, dkv_s, dkv_r,
 ):
     reps = n // hh
     lanes = 2 * width
@@ -67,12 +68,9 @@
     for k in range(1, n):
         pl.semaphore_signal(barrier, inc=1, device_id=(seq_at(k), mh), device_id_type=MESH)
         count += 1
-    for j in range(hh):
-        for d in range(1, nh):
-            pl.semaphore_signal(
-                barrier, inc=1, device_id=(seq_at(reps * j), head_at(d, -1)), device_id_type=MESH
-            )
-            count += 1
+    for d in range(1, nh):
+        pl.semaphore_signal(barrier, inc=1, device_id=(me, head_at(d, -1)), device_id_type=MESH)
+        count += 1
     loads[0].wait()
     for z in range(hh):
         kvstage[z] = kv_ref[:, z, :]
@@ -165,25 +163,17 @@
         p = (e * (1.0 / jnp.sum(e, axis=1, keepdims=True))).astype(BF16)
         probs[j * rows:(j + 1) * rows, :] = p
         att = dot(p, kvbuf[...])
-        att_out[j] = jnp.transpose(att)[width:].astype(BF16)
-        my_rows = pl.ds(pl.multiple_of(my_z * width, width), width)
-        for d in range(nh):
-            if d == 0 and j == 0:
-                attbuf[0, my_rows, :] = att_out[0]
-            else:
-                send(
-                    att_out.at[j], attbuf.at[d, my_rows], att_s.at[d, j], att_r.at[d, j],
-                    owner, head_at(d),
-                )
         dprob = dot(grad_rows.astype(BF16), kvt[...])
         grad_dot = jnp.sum(grad_rows * att.astype(BF16).astype(F32), axis=1, keepdims=True)
         ds = (p.astype(F32) * (dprob - grad_dot)).astype(BF16)
         dscore[j * rows:(j + 1) * rows, :] = ds
-        dq_out[j] = jnp.transpose(dot(ds, kvbuf[...]) * inv_root)[:width].astype(BF16)
+        home_out[j] = jnp.transpose(
+            jnp.where(low, dot(ds, kvbuf[...]) * inv_root, att)
+        ).astype(BF16)
         if j == 0:
-            dqbuf[my_rows, :] = dq_out[0]
+            homebuf[my_z] = home_out[0]
         else:
-            send(dq_out.at[j], dqbuf.at[my_rows], dq_s.at[j], dq_r.at[j], owner, mh)
+            send(home_out.at[j], homebuf.at[my_z], home_s.at[j], home_r.at[j], owner, mh)
         for i, d in ahead[j * len(ahead) // hh:(j + 1) * len(ahead) // hh]:
             forward(i, d)
 
@@ -199,19 +189,20 @@
         else:
             send(dkv_out.at[k], dkvbuf.at[k], dkv_s.at[k], dkv_r.at[k], seq_at(-k), mh)
 
-    def z_rows(j):
-        z = lax.rem(my_z + j, hh)
-        return pl.ds(pl.multiple_of(z * width, width), width)
-
     for j in range(1, hh):
-        arrived(dqbuf.at[z_rows(j)], dq_s.at[j], dq_r.at[j])
-    dq_ref[...] = dqbuf[...]
+        arrived(homebuf.at[lax.rem(my_z + j, hh)], home_s.at[j], home_r.at[j])
+    for z in range(hh):
+        at = slice(z * width, (z + 1) * width)
+        attbuf[0, at, :] = homebuf[z, width:lanes, :]
+    for d in range(nh - 1, 0, -1):
+        send(attbuf.at[0], attbuf.at[d], att_s.at[d], att_r.at[d], me, head_at(d))
+    for z in range(hh):
+        dq_ref[z * width:(z + 1) * width, :] = homebuf[z, 0:width, :]
 
     total = None
     for d in range(nh):
-        for j in range(hh):
-            if d or j:
-                arrived(attbuf.at[d, z_rows(j)], att_s.at[d, j], att_r.at[d, j])
+        if d:
+            arrived(attbuf.at[d], att_s.at[d], att_r.at[d])
         if d == 0:
             weight = w_ref[:, pl.ds(pl.multiple_of(mh * cols, cols), cols)]
         else:
@@ -274,10 +265,9 @@
             pltpu.VMEM((nh, hh * width, cols), BF16),
             pltpu.VMEM((hh * rows, n * rows), BF16),
             pltpu.VMEM((hh * rows, n * rows), BF16),
-            pltpu.VMEM((hh, width, rows), BF16),
             pltpu.VMEM((nh, hh * width, rows), BF16),
-            pltpu.VMEM((hh, width, rows), BF16),
-            pltpu.VMEM((hh * width, rows), BF16),
+            pltpu.VMEM((hh, lanes, rows), BF16),
+            pltpu.VMEM((hh, lanes, rows), BF16),
             pltpu.VMEM((n, rows, lanes), BF16),
             pltpu.VMEM((n, rows, lanes), BF16),
             dma((4,)),
@@ -285,12 +275,12 @@
             dma((nh, PIECES)), dma((nh, PIECES)),
             dma((nh, PIECES, reps)), dma((nh, PIECES, reps)),
             dma((hh,)), dma((hh,)),
-            dma((nh, hh)), dma((nh, hh)),
+            dma((nh,)), dma((nh,)),
             dma((hh,)), dma((hh,)),
             dma((n,)), dma((n,)),
         ],
         compiler_params=pltpu.CompilerParams(
-            collective_id=0, has_side_effects=True, vmem_limit_bytes=60 * 2**20
+            collective_id=0, has_side_effects=True, vmem_limit_bytes=VLIM * 2**16
         ),
     )(
         jnp.transpose(queries, (1, 2, 0)).reshape(hh * width, rows),

time: 41 us -> 37.6 us (0.917)
  Pallas kernels: 35.4 us -> 32 us
    pallas_call x1, Pallas kernels: 35.4 us -> 32 us  [fused_local(): pl.pallas_call(functools.partial(fused, n, nh, hh, rows, width, 1.0 / mat...]
where the time goes in v3:
time: 37.6 us; the launch traced here: 37.4 us
  Pallas kernels  32 us (85%)
  local copies, waits for them, and re-layouts  4.75 us (13%)
  between operations  0.64 us (2%)
    pallas_call x1, Pallas kernels, fused_local(): pl.pallas_call(functools.partial(fused, n, nh, hh, rows, width, 1.0 / mat...  32 us
    unnamed x3, local copies, waits for them, and re-layouts  4.75 us

profile of v3, /device:TPU:0, one launch (start us, length us, event | category | flops | bytes accessed | tf_op | source)
XLA Modules:
  0.0 37.4 jit_solution(8048589387115679537)
XLA Ops:
  0.6 32.0 %shard_map.76 = (bf16[128,1024]{1,0:T(8,128)(2,1)}, bf16[256,128]{1,0:T(8,128)(2,1)}, bf16[128,4,128]{2,1,0:T(4,128)(2,1)}) custom-call(bf16[256,128]{1,0:T(8,128)(2,1)} %bitcast.8, bf16[128,4,128]{2,1,0:T(4,128)(2,1)} %kv_hbm.1, bf16[256,4096]{1,0:T(8,128)(2,1)} %bitcast.7, bf16[128,4096]{1,0:T(8,128)(2,1)} %og_hbm.1, s32[8]{0:T(128)} %order_ref.1), custom_call_target="tpu_custom_call" | custom-call | tf_op jit(solution)/shard_map/pallas_call | solution.py:246
  32.6 1.7 %copy.11 = bf16[128,1024]{1,0:T(8,128)(2,1)} copy(bf16[128,1024]{1,0:T(8,128)(2,1)} %get-tuple-element.12) | data formatting | bytes 524288
  34.3 1.5 %copy.12 = bf16[128,4,64]{0,2,1:T(8,128)(2,1)} copy(bf16[128,4,64]{0,2,1:T(8,128)(2,1)} %bitcast.9) | data formatting | bytes 131072
  35.8 1.6 %copy.13 = bf16[128,4,128]{2,1,0:T(4,128)(2,1)} copy(bf16[128,4,128]{2,1,0:T(4,128)(2,1)} %get-tuple-element.14) | data formatting | bytes 262144
